TPU v7x, 32 devices: a whole 2x2x4 slice. The times are simulated.
32 devices in a mesh: group: 1, wide: 32 (over z, y, x, core).
Axes of the slice: x: 2, y: 2, z: 4, core: 2. Of those that a mesh axis runs over, the one named last changes fastest.
Arguments:
- resid: bfloat16 [32, 3072], P(('group', 'wide')), may hold values from -6 to 6
- query: bfloat16 [32, 4096], P(('group', 'wide')), may hold values from -4 to 4
- key: bfloat16 [32, 4096], P(('group', 'wide')), may hold values from -4 to 4
- value: bfloat16 [32, 4096], P(('group', 'wide')), may hold values from -6 to 6
- state: float32 [32, 32, 128, 128], P(('group', 'wide')), may hold values from -6 to 6
- decay: float32 [32], replicated, may hold values from 0.02 to 2
- out_gate: bfloat16 [32, 4096], P(('group', 'wide')), may hold values from -6 to 6
- norm_gain: float32 [4096], replicated, may hold values from 0.25 to 1.75
- w_out: bfloat16 [4096, 3072], P('wide'), may hold values from -0.09375 to 0.09375
- moe_gain: float32 [3072], replicated, may hold values from 0.25 to 1.75
- w_gate: bfloat16 [32, 576, 3072], P('wide'), may hold values from -0.109375 to 0.109375
- w_up: bfloat16 [32, 576, 3072], P('wide'), may hold values from -0.109375 to 0.109375
- w_down: bfloat16 [32, 576, 3072], P('wide'), may hold values from -0.09375 to 0.09375
- expert_ids: int32 [32, 2], P('group'), may hold values from 0 to 3, all different within a row; in each aligned block of 32 rows (0 to 31, 32 to 63, ...) at most 32 rows name the same one
- expert_weights: float32 [32, 2], P('group'), may hold values from 0.2 to 1
Outputs:
- mixed: bfloat16 [32, 3072], P(('group', 'wide'))
Inputs may be any that keep to these rules, and one draw needn't show every extreme that they name: `expert_ids`: each request names two different experts; every expert is named by some request; no expert is named by more than 32 requests, a bound that some block reaches.
All inputs are finite; a program needn't handle non-finite values.
Results may differ from a plain program's by a relative error of at most 0.012.
Values may be sent and summed in bfloat16 or wider, within the bound.
A program may use at most 64 MiB of HBM per device.

v0:
```python
import jax
import jax.numpy as jnp
from jax import lax
from jax.sharding import PartitionSpec as P

SPLIT = 8


def by_rows(left, weight):
    return lax.dot_general(
        left, weight, (((1,), (1,)), ((), ())), preferred_element_type=jnp.float32
    )


def shards(
    resid,
    query,
    key,
    value,
    state,
    decay,
    out_gate,
    norm_gain,
    w_out,
    moe_gain,
    w_gate,
    w_up,
    w_down,
    expert_ids,
    expert_weights,
):
    local_rows = resid.shape[0]
    heads = decay.shape[0]
    head_size = query.shape[1] // heads
    devices = lax.axis_size("wide")
    q_heads = query.astype(jnp.float32).reshape(local_rows, heads, head_size)
    k_heads = key.astype(jnp.float32).reshape(local_rows, heads, head_size)
    v_heads = value.astype(jnp.float32).reshape(local_rows, heads, head_size)
    fade = jnp.exp(-decay)
    new_state = fade[None, :, None, None] * state + jnp.einsum("rhi,rhj->rhij", k_heads, v_heads)
    att = jnp.einsum("rhi,rhij->rhj", q_heads, new_state).reshape(local_rows, heads * head_size)
    scale = lax.rsqrt(jnp.mean(att * att, axis=1, keepdims=True) + 1e-06)
    attn = (att * scale * norm_gain * jax.nn.sigmoid(out_gate.astype(jnp.float32))).astype(
        jnp.bfloat16
    )
    columns = lax.all_to_all(attn, "wide", split_axis=1, concat_axis=0, tiled=True)
    piece = columns
    proj = lax.psum_scatter(
        jnp.dot(piece, w_out, preferred_element_type=jnp.float32),
        "wide",
        scatter_dimension=0,
        tiled=True,
    )
    hid_res = (resid.astype(jnp.float32) + proj).astype(jnp.bfloat16)
    hid_f = hid_res.astype(jnp.float32)
    normed = (
        hid_f * lax.rsqrt(jnp.mean(hid_f * hid_f, axis=1, keepdims=True) + 1e-06) * moe_gain
    ).astype(jnp.bfloat16)
    all_inputs = lax.all_gather(normed, "wide", axis=0, tiled=True)
    owner = lax.axis_index("wide") // SPLIT
    weight_all = jnp.sum(jnp.where(expert_ids == owner, expert_weights, 0.0), axis=1)
    piece = all_inputs
    gate = by_rows(piece, w_gate[0])
    upper = by_rows(piece, w_up[0])
    inner = (jax.nn.silu(gate) * upper).astype(jnp.bfloat16)
    partial_value = (
        jnp.dot(inner, w_down[0], preferred_element_type=jnp.float32) * weight_all[:, None]
    ).reshape(devices, local_rows, hid_f.shape[1])
    returned = lax.all_to_all(partial_value, "wide", split_axis=0, concat_axis=0, tiled=True)
    experts_out = jnp.sum(returned, axis=0)
    return (hid_f + experts_out).astype(jnp.bfloat16)


def solution(mesh):
    return jax.shard_map(
        shards,
        mesh=mesh,
        in_specs=(
            P(("group", "wide"), None),
            P(("group", "wide"), None),
            P(("group", "wide"), None),
            P(("group", "wide"), None),
            P(("group", "wide"), None, None, None),
            P(),
            P(("group", "wide"), None),
            P(),
            P("wide", None),
            P(),
            P("wide", None, None),
            P("wide", None, None),
            P("wide", None, None),
            P("group", None),
            P("group", None),
        ),
        out_specs=P(("group", "wide"), None),
        check_vma=False,
    )
```

profile of v0, /device:TPU:0, one launch (start us, length us, event | category | flops | bytes accessed | tf_op | source)
XLA Modules:
  0.0 234.4 jit_solution(16891972919051586054)
XLA Ops:
  6.5 0.0 copy-start
  6.5 0.0 all-reduce.3.cloned.1.call-start
  6.5 0.8 negate_exponential_fusion
  7.3 0.9 convert.12
  8.3 0.7 convert.13
  9.0 2.3 %fusion.12 = f32[32,1,128]{2,1,0:T(1,128)S(1)} fusion(f32[1,32,128,128]{3,2,1,0:T(8,128)} %param.19, f32[32,128]{1,0:T(8,128)S(1)} %bitcast.58, f32[32,128]{1,0:T(8,128)S(1)} %bitcast.57, f32[32]{0:T(128)S(1)} %negate_exponential_fusion, bf16[1,4096]{1,0:T(2,128)(2,1)} %param.16), kind=kOutput, calls=%fused_computation.8 | convolution fusion | flops 2621440 | bytes 2154624 | tf_op jit(solution)/shard_map/rhi,rhij->rhj/dot_general | solution.py:41
  11.3 0.6 multiply_reduce_fusion
  12.7 0.7 bitcast_multiply_fusion
  13.4 0.8 convert_bitcast_fusion
  14.1 14.3 %all_to_all.21 = bf16[1,32,128]{2,0,1:T(2,128)(2,1)S(1)} all-to-all(bf16[1,32,128]{2,0,1:T(2,128)(2,1)S(1)} %convert_bitcast_fusion), channel_id=1, replica_groups=mesh['group'=1,'wide'=32] {'wide'}, dimensions={1} | all-to-all | bytes 16384 | tf_op jit(solution)/shard_map/all_to_all | solution.py:46
  28.4 2.1 fusion.42
  30.5 0.0 all-reduce.3.cloned.1.call-update
  30.6 0.7 fusion.45
  31.3 123.3 %all-reduce.3.cloned.1.call-done = f32[32,3072]{1,0:T(8,128)} async-done(((f32[32,3072]{1,0:T(8,128)}), f32[32,3072]{1,0:T(8,128)}) %all-reduce.3.cloned.1.call-update) | async-done | bytes 393232
  154.6 1.5 multiply_reduce_fusion.1
  156.8 0.7 convert_bitcast_fusion.1
  157.5 40.7 %all-gather = bf16[32,1,3072]{2,1,0:T(2,128)(2,1)S(1)} all-gather(bf16[1,1,3072]{2,1,0:T(2,128)(2,1)S(1)} %convert_bitcast_fusion.1), channel_id=1, replica_groups=mesh['group'=1,'wide'=32] {'wide'}, dimensions={0}, use_global_device_ids=true | all-gather | bytes 202752 | tf_op jit(solution)/shard_map/all_gather | solution.py:59
  198.2 0.0 copy-start.1
  198.2 0.7 copy-done.1
  199.0 3.8 %fusion.4 = f32[32,576]{1,0:T(8,128)} fusion(bf16[1,576,3072]{2,1,0:T(8,128)(2,1)} %param.25, bf16[32,1,3072]{2,1,0:T(2,128)(2,1)S(1)} %all-gather), kind=kOutput, calls=%fused_computation.4 | convolution fusion | flops 113246208 | bytes 3809280 | tf_op jit(solution)/shard_map/dot_general | solution.py:10
  202.7 0.0 copy-done
  202.7 4.7 %fusion.9 = f32[32,1,3072]{2,0,1:T(8,128)} fusion(bf16[1,576,3072]{2,1,0:T(8,128)(2,1)S(1)} %copy-done, bf16[1,576,3072]{2,1,0:T(8,128)(2,1)} %param.26, f32[32]{0:T(128)S(1)} %fusion.45, f32[32,576]{1,0:T(8,128)} %fusion.4, bf16[32,1,3072]{2,1,0:T(2,128)(2,1)} %copy-done.1), kind=kOutput, calls=%fused_computation.7 | convolution fusion | flops 226701312 | bytes 7741568 | tf_op jit(solution)/shard_map/dot_general | solution.py:67
  207.4 1.4 copy.18
  208.8 15.6 %all_to_all.22 = f32[32,1,3072]{2,1,0:T(1,128)} all-to-all(f32[32,1,3072]{2,1,0:T(1,128)S(1)} %copy.18), channel_id=1, replica_groups=mesh['group'=1,'wide'=32] {'wide'}, dimensions={0} | all-to-all | bytes 786432 | tf_op jit(solution)/shard_map/all_to_all | solution.py:69
  224.4 1.8 reduce_sum.41
  226.2 1.3 add_convert_fusion
Async XLA Ops:
  6.5 196.2 %copy-start = (bf16[1,576,3072]{2,1,0:T(8,128)(2,1)S(1)}, bf16[1,576,3072]{2,1,0:T(8,128)(2,1)}, u32[]{:S(2)}) copy-start(bf16[1,576,3072]{2,1,0:T(8,128)(2,1)} %param.27) | copy-start | bytes 10616836
  6.5 148.0 %all-reduce.3.cloned.1.call-start = ((), (), s32[]{:S(2)}) async-start(), calls=%async_computation.2 | async-start | bytes 786432
  198.2 0.7 copy-start.1
Sparse Core Ops, SparseCore 0:
  30.7 123.8 all-reduce.2
where the time goes:
time: 235 us; the launch traced here: 234 us
  waiting for transfers between devices  123 us (52%)
  blocking collectives  70.5 us (30%)
  between operations  14.8 us (6%)
  matrix products  12.9 us (5%)
  other arithmetic  10.7 us (5%)
    unnamed x2, waiting for transfers between devices  123 us
    all_gather x1, blocking collectives, shards(): all_inputs = lax.all_gather(normed, 'wide', axis=0, tiled=True)  40.7 us
    all_to_all x1, blocking collectives, shards(): lax.all_to_all(partial_value, 'wide', split_axis=0, concat_axis=0, tiled=...  15.6 us
    all_to_all x1, blocking collectives, shards(): lax.all_to_all(attn, 'wide', split_axis=1, concat_axis=0, tiled=True)  14.3 us
  transfers between devices with their start and end apart: 1, of which 1 were waited for; matrix products, arithmetic and copies ran while one was open for 0% of the time, Pallas kernels for 0%

commit v1 on v0

v1 whole, which is shorter than its diff:
```python
import functools

import jax
import jax.numpy as jnp
from jax import lax
from jax.experimental import pallas as pl
from jax.experimental.pallas import tpu as pltpu
from jax.sharding import PartitionSpec as P

F32, BF16 = jnp.float32, jnp.bfloat16
TILE = 16
STATE_CUTS = 4
VMEM = 44 * 1024 * 1024


def iota(shape, dim):
    return lax.broadcasted_iota(jnp.int32, shape, dim)


def dot(left, right):
    return jnp.dot(left, right, preferred_element_type=F32)


def by_rows(left, weight):
    return lax.dot_general(left, weight, (((1,), (1,)), ((), ())), preferred_element_type=F32)


def layout(n, width):
    inner = 1
    while inner * inner < n:
        inner *= 2
    outer = n // inner
    pieces = max(1, TILE // outer)
    columns = width // pieces
    chunks = max(c for c in (1, 2, 3, 4) if (columns // 128) % c == 0)
    return inner, outer, pieces, columns, chunks


def kernel(
    n, slab_split,
    resid, query, key, value, decay, out_gate, norm_gain, moe_gain, ids, weights,
    state_h, w_out_h, w_gate_h, w_up_h, w_down_h,
    out,
    state, w_out, w_gate, w_up, w_down,
    heads5, rows2, att3, recv1, send_a, recv_a, send_b, recv_b, recv_c, recv_d,
    xs, send_e, recv_e, send_f, recv_f,
    load_sem, send_sem, recv_sem, chunk_send, chunk_recv, last_send, last_recv,
):
    heads, hdim = att3.shape[0], att3.shape[2]
    width = resid.shape[1]
    inner, outer, pieces, columns, chunks = layout(n, width)
    step = columns // chunks
    share = w_out_h.shape[0]
    me = lax.axis_index("wide")
    a, b = me // inner, me % inner
    tile = outer * pieces

    barrier = pltpu.get_barrier_semaphore()

    def greet(i, carry):
        pl.semaphore_signal(
            barrier, inc=1, device_id={"wide": (me + i) % n},
            device_id_type=pl.DeviceIdType.MESH,
        )
        return carry

    part = state.shape[0] // STATE_CUTS
    loads = []
    for c in range(STATE_CUTS):
        at = pl.ds(c * part, part)
        loads.append(pltpu.make_async_copy(state_h.at[at], state.at[at], load_sem.at[c]))
        loads[-1].start()
    if share == hdim:
        get_out = pltpu.make_async_copy(w_out_h, w_out, load_sem.at[STATE_CUTS])
    else:
        w_out[...] = jnp.zeros_like(w_out)
        place = pl.ds(pl.multiple_of((me * share) % hdim, share), share)
        get_out = pltpu.make_async_copy(w_out_h, w_out.at[place], load_sem.at[STATE_CUTS])
    get_out.start()
    big = []
    for i, (src, dst) in enumerate(((w_gate_h, w_gate), (w_up_h, w_up), (w_down_h, w_down))):
        big.append(pltpu.make_async_copy(src.at[0], dst, load_sem.at[STATE_CUTS + 1 + i]))
        big[-1].start()

    lax.fori_loop(1, n, greet, 0)

    for i, ref in enumerate((query, key, value, out_gate, norm_gain)):
        line = ref[...].astype(F32)
        for h in range(heads):
            heads5[i, h : h + 1, :] = line[:, h * hdim : (h + 1) * hdim]
    for i, ref in enumerate((resid, moe_gain)):
        line = ref[...].astype(F32)
        for p in range(pieces):
            rows2[i, p : p + 1, :] = line[:, p * columns : (p + 1) * columns]
    q, k, v = heads5[0], heads5[1], heads5[2]
    head_of = iota((heads, hdim), 0)
    eye = iota((heads, heads), 0) == iota((heads, heads), 1)
    fade = jnp.sum(
        jnp.where(eye, jnp.broadcast_to(jnp.exp(-decay[...]), (heads, heads)), 0.0),
        axis=1, keepdims=True,
    )
    att = jnp.zeros((heads, hdim), F32)
    per_cut = heads // STATE_CUTS
    for c in range(STATE_CUTS):
        diagonal = jnp.concatenate(
            [jnp.where(head_of == c * per_cut + h, q, 0.0).astype(BF16) for h in range(per_cut)],
            axis=1,
        )
        loads[c].wait()
        att += dot(diagonal, state[pl.ds(c * part, part), :].astype(BF16))
    att = fade * att + jnp.sum(q * k, axis=1, keepdims=True) * v
    mean = jnp.sum(jnp.sum(att * att, axis=1, keepdims=True), axis=0, keepdims=True) / (
        heads * hdim
    )
    attn = att * lax.rsqrt(mean + 1e-06) * heads5[4] * jax.nn.sigmoid(heads5[3])
    att3[...] = attn.reshape(heads, 1, hdim)

    pl.semaphore_wait(barrier, n - 1)

    slot = b * outer + a

    def send_head(i, carry):
        peer = (me + i) % n
        pltpu.make_async_remote_copy(
            src_ref=att3.at[(peer * share) // hdim], dst_ref=recv1.at[slot],
            send_sem=send_sem.at[0], recv_sem=recv_sem.at[0],
            device_id={"wide": peer}, device_id_type=pl.DeviceIdType.MESH,
        ).start()
        return carry

    lax.fori_loop(1, n, send_head, 0)
    recv1[slot] = att3[(me * share) // hdim]

    def settle(ref, count, sem):
        view = ref.at[pl.ds(0, count)]
        pltpu.make_async_copy(view, view, sem).wait()

    def to_inner(src, dst, ssem, rsem, pick):
        def one(i, carry):
            peer = (b + i) % inner
            pltpu.make_async_remote_copy(
                src_ref=src.at[peer if pick else b], dst_ref=dst.at[b],
                send_sem=ssem, recv_sem=rsem,
                device_id={"wide": a * inner + peer}, device_id_type=pl.DeviceIdType.MESH,
            ).start()
            return carry

        lax.fori_loop(1, inner, one, 0)

    def to_outer(src, dst, ssem, rsem, pick):
        def one(i, carry):
            peer = (a + i) % outer
            pltpu.make_async_remote_copy(
                src_ref=src.at[peer if pick else a], dst_ref=dst.at[a],
                send_sem=ssem, recv_sem=rsem,
                device_id={"wide": peer * inner + b}, device_id_type=pl.DeviceIdType.MESH,
            ).start()
            return carry

        lax.fori_loop(1, outer, one, 0)

    lines = n * pieces
    spread = (iota((lines, n), 0) // pieces == iota((lines, n), 1)).astype(F32).astype(BF16)
    piece_of = iota((lines, 1), 0) % pieces

    def only(p, full):
        return jnp.where(piece_of == p, full, 0.0).astype(BF16)

    owner = me // slab_split
    coef = jnp.sum(jnp.where(ids[...] == owner, weights[...], 0.0), axis=1, keepdims=True)
    line = iota((n, lines), 1) // pieces
    request = (line % outer) * inner + line // outer
    coef_row = jnp.sum(
        jnp.where(request == iota((n, lines), 0), jnp.broadcast_to(coef, (n, lines)), 0.0),
        axis=0, keepdims=True,
    )
    same = iota((lines, lines), 0) == iota((lines, lines), 1)
    coef_line = jnp.sum(
        jnp.where(same, jnp.broadcast_to(coef_row, (lines, lines)), 0.0), axis=1, keepdims=True
    )

    get_out.wait()
    settle(recv1, n - 1, recv_sem.at[0])
    full = dot(spread, recv1[...].reshape(n, hdim).astype(BF16))
    proj = jnp.zeros((lines, columns), F32)
    for p in range(pieces):
        proj += dot(only(p, full), w_out[:, p * columns : (p + 1) * columns])
    send_a[...] = proj.astype(BF16).reshape(inner, tile, columns)
    to_inner(send_a, recv_a, send_sem.at[1], recv_sem.at[1], True)
    recv_a[b] = send_a[b]
    settle(recv_a, inner - 1, recv_sem.at[1])
    total = recv_a[0].astype(F32)
    for i in range(1, inner):
        total += recv_a[i].astype(F32)
    send_b[...] = total.reshape(outer, pieces, columns)
    to_outer(send_b, recv_b, send_sem.at[2], recv_sem.at[2], True)
    recv_b[a] = send_b[a]
    settle(recv_b, outer - 1, recv_sem.at[2])
    hid = (rows2[0] + jnp.sum(recv_b[...], axis=0)).astype(BF16).astype(F32)
    mean = jnp.sum(jnp.sum(hid * hid, axis=1, keepdims=True), axis=0, keepdims=True) / width
    recv_c[a] = hid * lax.rsqrt(mean + 1e-06) * rows2[1]

    to_outer(recv_c, recv_c, send_sem.at[3], recv_sem.at[3], False)
    settle(recv_c, outer - 1, recv_sem.at[3])
    recv_d[b] = recv_c[...].reshape(tile, columns).astype(BF16)
    to_inner(recv_d, recv_d, send_sem.at[4], recv_sem.at[4], False)
    settle(recv_d, inner - 1, recv_sem.at[4])
    normed = recv_d[...].reshape(lines, columns)
    at_line = iota((n, lines), 0) * pieces
    for p in range(pieces):
        pick = (iota((n, lines), 1) == at_line + p).astype(F32).astype(BF16)
        xs[p] = dot(pick, normed).astype(BF16)

    big[0].wait()
    big[1].wait()
    hidden = w_gate.shape[0]

    def piece(p, carry):
        gate, upper = carry
        at = pl.ds(pl.multiple_of(p * columns, columns), columns)
        x = xs[p]
        return gate + by_rows(x, w_gate[:, at]), upper + by_rows(x, w_up[:, at])

    zero = jnp.zeros((n, hidden), F32)
    gate, upper = lax.fori_loop(0, pieces, piece, (zero, zero))
    inner_act = (gate * jax.nn.sigmoid(gate) * upper).astype(BF16)
    full = dot(spread, inner_act)
    big[2].wait()
    for j in range(chunks):
        acc = jnp.zeros((lines, step), F32)
        for p in range(pieces):
            start = p * columns + j * step
            acc += dot(only(p, full), w_down[:, start : start + step])
        send_e[j] = (acc * coef_line).astype(BF16).reshape(inner, tile, step)
        to_inner(send_e.at[j], recv_e.at[j], chunk_send.at[j], chunk_recv.at[j], True)
        recv_e[j, b] = send_e[j, b]
    for j in range(chunks):
        settle(recv_e.at[j], inner - 1, chunk_recv.at[j])
        total = recv_e[j, 0].astype(F32)
        for i in range(1, inner):
            total += recv_e[j, i].astype(F32)
        send_f[j] = total.reshape(outer, pieces, step)
        to_outer(send_f.at[j], recv_f.at[j], last_send.at[j], last_recv.at[j], True)
        recv_f[j, a] = send_f[j, a]
    for j in range(chunks):
        settle(recv_f.at[j], outer - 1, last_recv.at[j])
        mixed = (hid[:, j * step : (j + 1) * step] + jnp.sum(recv_f[j], axis=0)).astype(BF16)
        for p in range(pieces):
            start = p * columns + j * step
            out[:, start : start + step] = mixed[p : p + 1, :]

    settle(recv1, n - 1, send_sem.at[0])
    settle(send_a, inner - 1, send_sem.at[1])
    settle(send_b, outer - 1, send_sem.at[2])
    settle(recv_c, outer - 1, send_sem.at[3])
    settle(recv_d, inner - 1, send_sem.at[4])
    for j in range(chunks):
        settle(send_e.at[j], inner - 1, chunk_send.at[j])
        settle(send_f.at[j], outer - 1, last_send.at[j])


def shards(
    resid, query, key, value, state, decay, out_gate, norm_gain, w_out, moe_gain,
    w_gate, w_up, w_down, expert_ids, expert_weights, *, slab_split,
):
    n = lax.axis_size("wide")
    width = resid.shape[1]
    heads, hdim = state.shape[1], state.shape[2]
    inner, outer, pieces, columns, chunks = layout(n, width)
    step = columns // chunks
    tile = outer * pieces
    hidden = w_gate.shape[1]
    vmem = pl.BlockSpec(memory_space=pltpu.VMEM)
    hbm = pl.BlockSpec(memory_space=pl.ANY)
    sems = pltpu.SemaphoreType.DMA
    return pl.pallas_call(
        functools.partial(kernel, n, slab_split),
        out_shape=jax.ShapeDtypeStruct(resid.shape, resid.dtype),
        in_specs=[vmem] * 10 + [hbm] * 5,
        out_specs=vmem,
        scratch_shapes=[
            pltpu.VMEM((heads * hdim, hdim), F32),
            pltpu.VMEM((hdim, width), BF16),
            pltpu.VMEM((hidden, width), BF16),
            pltpu.VMEM((hidden, width), BF16),
            pltpu.VMEM((hidden, width), BF16),
            pltpu.VMEM((5, heads, hdim), F32),
            pltpu.VMEM((2, pieces, columns), F32),
            pltpu.VMEM((heads, 1, hdim), F32),
            pltpu.VMEM((n, 1, hdim), F32),
            pltpu.VMEM((inner, tile, columns), BF16),
            pltpu.VMEM((inner, tile, columns), BF16),
            pltpu.VMEM((outer, pieces, columns), F32),
            pltpu.VMEM((outer, pieces, columns), F32),
            pltpu.VMEM((outer, pieces, columns), F32),
            pltpu.VMEM((inner, tile, columns), BF16),
            pltpu.VMEM((pieces, n, columns), BF16),
            pltpu.VMEM((chunks, inner, tile, step), BF16),
            pltpu.VMEM((chunks, inner, tile, step), BF16),
            pltpu.VMEM((chunks, outer, pieces, step), F32),
            pltpu.VMEM((chunks, outer, pieces, step), F32),
            sems((STATE_CUTS + 4,)),
            sems((5,)),
            sems((5,)),
            sems((chunks,)),
            sems((chunks,)),
            sems((chunks,)),
            sems((chunks,)),
        ],
        compiler_params=pltpu.CompilerParams(
            collective_id=0, has_side_effects=True, vmem_limit_bytes=VMEM
        ),
        name="decode_layer",
    )(
        resid, query, key, value, decay.reshape(1, -1), out_gate, norm_gain.reshape(1, -1),
        moe_gain.reshape(1, -1), expert_ids, expert_weights,
        state.reshape(heads * hdim, hdim), w_out, w_gate, w_up, w_down,
    )


SPLIT = 8


def solution(mesh):
    rows = P(("group", "wide"), None)
    return jax.shard_map(
        functools.partial(shards, slab_split=SPLIT),
        mesh=mesh,
        in_specs=(
            rows, rows, rows, rows,
            P(("group", "wide"), None, None, None),
            P(), rows, P(), P("wide", None), P(),
            P("wide", None, None), P("wide", None, None), P("wide", None, None),
            P("group", None), P("group", None),
        ),
        out_specs=rows,
        check_vma=False,
    )
```

time: 235 us -> 54.8 us (0.23)
  waiting for transfers between devices: 123 us -> 0 us
  blocking collectives: 70.5 us -> 0 us
  Pallas kernels: 0 us -> 39.5 us
  between operations: 14.8 us -> 0.02 us
  matrix products: 12.9 us -> 0 us
  local copies, waits for them, and re-layouts: 2.14 us -> 14.5 us
  other arithmetic: 10.7 us -> 0 us
    unnamed x2 -> x0, waiting for transfers between devices: 123 us -> none
    all_gather x1 -> x0, blocking collectives: 40.7 us -> none  [shards(): all_inputs = lax.all_gather(normed, 'wide', axis=0, tiled=True)]
    pallas_call x0 -> x1, Pallas kernels: none -> 39.5 us  [shards(): pl.pallas_call(functools.partial(kernel, n, slab_split), out_shape=jax.Sh...]
    all_to_all x2 -> x0, blocking collectives: 29.8 us -> none  [the longest x1 15.6 us: shards(): lax.all_to_all(partial_value, 'wide', split_axis=0, concat_axis=0, tiled=...]
    unnamed x4 -> x27, local copies, waits for them, and re-layouts: 0.74 us -> 14.5 us
    dot_general x4 -> x0, matrix products: 12.9 us -> none  [the longest x1 4.67 us: shards(): jnp.dot(inner, w_down[0], preferred_element_type=jnp.float32)]
    reduce_sum x4 -> x0, other arithmetic: 4.68 us -> none  [the longest x1 1.82 us: shards(): experts_out = jnp.sum(returned, axis=0)]
  transfers between devices with their start and end apart: 1 -> 0, of which waited for: 1 -> 0; matrix products, arithmetic and copies ran while one was open for 0% -> 0% of each run, Pallas kernels for 0% -> 0%
where the time goes in v1:
time: 54.8 us; the launch traced here: 54 us
  Pallas kernels  39.5 us (72%)
  local copies, waits for them, and re-layouts  14.5 us (26%)
    pallas_call x1, Pallas kernels, shards(): pl.pallas_call(functools.partial(kernel, n, slab_split), out_shape=jax.Sh...  39.5 us
    unnamed x27, local copies, waits for them, and re-layouts  14.5 us

profile of v1, /device:TPU:0, one launch (start us, length us, event | category | flops | bytes accessed | tf_op | source)
XLA Modules:
  0.0 54.0 jit_solution(10877349331703212907)
XLA Ops:
  0.0 0.8 %copy.16.ids = s32[32,2]{1,0:T(8,128)S(1)} copy(s32[32,2]{0,1:T(2,128)} %param.28) | data formatting | bytes 512 | tf_op args[13]
  0.8 0.8 %copy.17.weights = f32[32,2]{1,0:T(8,128)S(1)} copy(f32[32,2]{0,1:T(2,128)} %param.29) | data formatting | bytes 512 | tf_op args[14]
  1.5 0.0 copy-start
  1.5 2.0 %copy-done = bf16[1,576,3072]{2,1,0:T(8,128)(2,1)S(1)} copy-done((bf16[1,576,3072]{2,1,0:T(8,128)(2,1)S(1)}, bf16[1,576,3072]{2,1,0:T(8,128)(2,1)}, u32[]{:S(2)}) %copy-start) | copy-done | bytes 3538968
  3.5 0.0 copy-start.1
  3.5 2.0 %copy-done.1 = bf16[1,576,3072]{2,1,0:T(8,128)(2,1)S(1)} copy-done((bf16[1,576,3072]{2,1,0:T(8,128)(2,1)S(1)}, bf16[1,576,3072]{2,1,0:T(8,128)(2,1)}, u32[]{:S(2)}) %copy-start.1) | copy-done | bytes 3538968
  5.5 0.0 copy-start.2
  5.5 1.6 %copy-done.2 = f32[1,32,128,128]{3,2,1,0:T(8,128)S(1)} copy-done((f32[1,32,128,128]{3,2,1,0:T(8,128)S(1)}, f32[1,32,128,128]{3,2,1,0:T(8,128)}, u32[]{:S(2)}) %copy-start.2) | copy-done | bytes 2097176
  7.1 0.0 copy-start.3
  7.1 1.1 %copy-done.3 = bf16[128,3072]{1,0:T(8,128)(2,1)S(1)} copy-done((bf16[128,3072]{1,0:T(8,128)(2,1)S(1)}, bf16[128,3072]{1,0:T(8,128)(2,1)}, u32[]{:S(2)}) %copy-start.3) | copy-done | bytes 786456
  8.2 0.0 copy-start.4
  8.2 0.7 %copy-done.4 = bf16[1,4096]{1,0:T(2,128)(2,1)S(1)} copy-done((bf16[1,4096]{1,0:T(2,128)(2,1)S(1)}, bf16[1,4096]{1,0:T(2,128)(2,1)}, u32[]{:S(2)}) %copy-start.4) | copy-done | bytes 8216
  9.0 0.0 copy-start.5
  9.0 0.7 %copy-done.5 = bf16[1,4096]{1,0:T(2,128)(2,1)S(1)} copy-done((bf16[1,4096]{1,0:T(2,128)(2,1)S(1)}, bf16[1,4096]{1,0:T(2,128)(2,1)}, u32[]{:S(2)}) %copy-start.5) | copy-done | bytes 8216
  9.7 0.0 copy-start.6
  9.7 0.7 %copy-done.6 = bf16[1,4096]{1,0:T(2,128)(2,1)S(1)} copy-done((bf16[1,4096]{1,0:T(2,128)(2,1)S(1)}, bf16[1,4096]{1,0:T(2,128)(2,1)}, u32[]{:S(2)}) %copy-start.6) | copy-done | bytes 8216
  10.4 0.0 copy-start.7
  10.4 0.7 %copy-done.7 = bf16[1,4096]{1,0:T(2,128)(2,1)S(1)} copy-done((bf16[1,4096]{1,0:T(2,128)(2,1)S(1)}, bf16[1,4096]{1,0:T(2,128)(2,1)}, u32[]{:S(2)}) %copy-start.7) | copy-done | bytes 8216
  11.1 0.0 copy-start.8
  11.1 0.7 %copy-done.8 = f32[4096]{0:T(1024)S(1)} copy-done((f32[4096]{0:T(1024)S(1)}, f32[4096]{0:T(1024)}, u32[]{:S(2)}) %copy-start.8) | copy-done | bytes 16408
  11.8 0.0 copy-start.9
  11.8 0.7 %copy-done.9 = bf16[1,3072]{1,0:T(2,128)(2,1)S(1)} copy-done((bf16[1,3072]{1,0:T(2,128)(2,1)S(1)}, bf16[1,3072]{1,0:T(2,128)(2,1)}, u32[]{:S(2)}) %copy-start.9) | copy-done | bytes 6168
  12.5 0.0 copy-start.10
  12.5 0.7 %copy-done.10 = f32[3072]{0:T(1024)S(1)} copy-done((f32[3072]{0:T(1024)S(1)}, f32[3072]{0:T(1024)}, u32[]{:S(2)}) %copy-start.10) | copy-done | bytes 12312
  13.3 0.0 copy-start.11
  13.3 0.7 %copy-done.11 = f32[32]{0:T(128)S(1)} copy-done((f32[32]{0:T(128)S(1)}, f32[32]{0:T(128)}, u32[]{:S(2)}) %copy-start.11) | copy-done | bytes 152
  13.9 39.5 %decode_layer.1 = bf16[1,3072]{1,0:T(2,128)(2,1)S(1)} custom-call(bf16[1,3072]{1,0:T(2,128)(2,1)S(1)} %copy-done.9, bf16[1,4096]{1,0:T(2,128)(2,1)S(1)} %copy-done.4, bf16[1,4096]{1,0:T(2,128)(2,1)S(1)} %copy-done.5, bf16[1,4096]{1,0:T(2,128)(2,1)S(1)} %copy-done.6, f32[1,32]{1,0:T(1,128)S(1)} %bitcast.7, bf16[1,4096]{1,0:T(2,128)(2,1)S(1)} %copy-done.7, ...), custom_call_target="tpu_custom_call" | custom-call | tf_op jit(solution)/shard_map/decode_layer/pallas_call | solution.py:276
  53.4 0.6 %copy.19 = bf16[1,3072]{1,0:T(2,128)(2,1)} copy(bf16[1,3072]{1,0:T(2,128)(2,1)S(1)} %decode_layer.1) | data formatting | bytes 12288
Async XLA Ops:
  1.5 2.0 %copy-start = (bf16[1,576,3072]{2,1,0:T(8,128)(2,1)S(1)}, bf16[1,576,3072]{2,1,0:T(8,128)(2,1)}, u32[]{:S(2)}) copy-start(bf16[1,576,3072]{2,1,0:T(8,128)(2,1)} %w_gate_h.1) | copy-start | bytes 10616836
  3.5 2.0 %copy-start.1 = (bf16[1,576,3072]{2,1,0:T(8,128)(2,1)S(1)}, bf16[1,576,3072]{2,1,0:T(8,128)(2,1)}, u32[]{:S(2)}) copy-start(bf16[1,576,3072]{2,1,0:T(8,128)(2,1)} %w_up_h.1) | copy-start | bytes 10616836
  5.5 1.6 %copy-start.2 = (f32[1,32,128,128]{3,2,1,0:T(8,128)S(1)}, f32[1,32,128,128]{3,2,1,0:T(8,128)}, u32[]{:S(2)}) copy-start(f32[1,32,128,128]{3,2,1,0:T(8,128)} %param.19) | copy-start | bytes 6291460
  7.1 1.1 %copy-start.3 = (bf16[128,3072]{1,0:T(8,128)(2,1)S(1)}, bf16[128,3072]{1,0:T(8,128)(2,1)}, u32[]{:S(2)}) copy-start(bf16[128,3072]{1,0:T(8,128)(2,1)} %w_out_h.1) | copy-start | bytes 2359300
  8.2 0.7 %copy-start.4 = (bf16[1,4096]{1,0:T(2,128)(2,1)S(1)}, bf16[1,4096]{1,0:T(2,128)(2,1)}, u32[]{:S(2)}) copy-start(bf16[1,4096]{1,0:T(2,128)(2,1)} %query.1) | copy-start | bytes 24580
  9.0 0.7 %copy-start.5 = (bf16[1,4096]{1,0:T(2,128)(2,1)S(1)}, bf16[1,4096]{1,0:T(2,128)(2,1)}, u32[]{:S(2)}) copy-start(bf16[1,4096]{1,0:T(2,128)(2,1)} %key.1) | copy-start | bytes 24580
  9.7 0.7 %copy-start.6 = (bf16[1,4096]{1,0:T(2,128)(2,1)S(1)}, bf16[1,4096]{1,0:T(2,128)(2,1)}, u32[]{:S(2)}) copy-start(bf16[1,4096]{1,0:T(2,128)(2,1)} %value.1) | copy-start | bytes 24580
  10.4 0.7 %copy-start.7 = (bf16[1,4096]{1,0:T(2,128)(2,1)S(1)}, bf16[1,4096]{1,0:T(2,128)(2,1)}, u32[]{:S(2)}) copy-start(bf16[1,4096]{1,0:T(2,128)(2,1)} %out_gate.1) | copy-start | bytes 24580
  11.1 0.7 %copy-start.8 = (f32[4096]{0:T(1024)S(1)}, f32[4096]{0:T(1024)}, u32[]{:S(2)}) copy-start(f32[4096]{0:T(1024)} %param.22) | copy-start | bytes 49156
  11.8 0.7 %copy-start.9 = (bf16[1,3072]{1,0:T(2,128)(2,1)S(1)}, bf16[1,3072]{1,0:T(2,128)(2,1)}, u32[]{:S(2)}) copy-start(bf16[1,3072]{1,0:T(2,128)(2,1)} %resid.1) | copy-start | bytes 18436
  12.5 0.7 %copy-start.10 = (f32[3072]{0:T(1024)S(1)}, f32[3072]{0:T(1024)}, u32[]{:S(2)}) copy-start(f32[3072]{0:T(1024)} %param.24) | copy-start | bytes 36868
  13.3 0.7 %copy-start.11 = (f32[32]{0:T(128)S(1)}, f32[32]{0:T(128)}, u32[]{:S(2)}) copy-start(f32[32]{0:T(128)} %param.20) | copy-start | bytes 388

commit v2 on v1

--- a/solution.py
+++ b/solution.py
@@ -10,7 +10,7 @@
 F32, BF16 = jnp.float32, jnp.bfloat16
 TILE = 16
 STATE_CUTS = 4
-VMEM = 44 * 1024 * 1024
+VMEM = 63 * 1024 * 1024
 
 
 def iota(shape, dim):
@@ -38,13 +38,14 @@
 
 def kernel(
     n, slab_split,
-    resid, query, key, value, decay, out_gate, norm_gain, moe_gain, ids, weights,
+    resid_h, query_h, key_h, value_h, decay_h, out_gate_h, norm_gain_h, moe_gain_h, ids_h, weights_h,
     state_h, w_out_h, w_gate_h, w_up_h, w_down_h,
     out,
+    resid, query, key, value, decay, out_gate, norm_gain, moe_gain, ids, weights,
     state, w_out, w_gate, w_up, w_down,
-    heads5, rows2, att3, recv1, send_a, recv_a, send_b, recv_b, recv_c, recv_d,
+    heads5, gains, hids, att3, recv1, send_a, recv_a, recv_r, recv_b, recv_d,
     xs, send_e, recv_e, send_f, recv_f,
-    load_sem, send_sem, recv_sem, chunk_send, chunk_recv, last_send, last_recv,
+    small_sem, load_sem, send_sem, recv_sem, chunk_send, chunk_recv, last_send, last_recv,
 ):
     heads, hdim = att3.shape[0], att3.shape[2]
     width = resid.shape[1]
@@ -64,6 +65,14 @@
         )
         return carry
 
+    small = []
+    for i, (src, dst) in enumerate((
+        (query_h, query), (key_h, key), (value_h, value), (out_gate_h, out_gate),
+        (norm_gain_h, norm_gain), (decay_h, decay), (resid_h, resid),
+        (moe_gain_h, moe_gain), (ids_h, ids), (weights_h, weights),
+    )):
+        small.append(pltpu.make_async_copy(src, dst, small_sem.at[i]))
+        small[-1].start()
     part = state.shape[0] // STATE_CUTS
     loads = []
     for c in range(STATE_CUTS):
@@ -84,14 +93,18 @@
 
     lax.fori_loop(1, n, greet, 0)
 
+    for copy in small:
+        copy.wait()
     for i, ref in enumerate((query, key, value, out_gate, norm_gain)):
         line = ref[...].astype(F32)
         for h in range(heads):
             heads5[i, h : h + 1, :] = line[:, h * hdim : (h + 1) * hdim]
-    for i, ref in enumerate((resid, moe_gain)):
-        line = ref[...].astype(F32)
-        for p in range(pieces):
-            rows2[i, p : p + 1, :] = line[:, p * columns : (p + 1) * columns]
+    line = resid[...].astype(F32)
+    for p in range(pieces):
+        recv_r[a, p : p + 1, :] = line[:, p * columns : (p + 1) * columns]
+        for i in range(outer):
+            at = i * pieces + p
+            gains[at : at + 1, :] = moe_gain[:, p * columns : (p + 1) * columns]
     q, k, v = heads5[0], heads5[1], heads5[2]
     head_of = iota((heads, hdim), 0)
     eye = iota((heads, heads), 0) == iota((heads, heads), 1)
@@ -167,17 +180,15 @@
         return jnp.where(piece_of == p, full, 0.0).astype(BF16)
 
     owner = me // slab_split
-    coef = jnp.sum(jnp.where(ids[...] == owner, weights[...], 0.0), axis=1, keepdims=True)
-    line = iota((n, lines), 1) // pieces
+    coef = jnp.sum(jnp.where(ids[...] == owner, weights[...], 0.0), axis=0, keepdims=True)
+    line = iota((lines, n), 0) // pieces
     request = (line % outer) * inner + line // outer
-    coef_row = jnp.sum(
-        jnp.where(request == iota((n, lines), 0), jnp.broadcast_to(coef, (n, lines)), 0.0),
-        axis=0, keepdims=True,
-    )
-    same = iota((lines, lines), 0) == iota((lines, lines), 1)
     coef_line = jnp.sum(
-        jnp.where(same, jnp.broadcast_to(coef_row, (lines, lines)), 0.0), axis=1, keepdims=True
-    )
+        jnp.where(request == iota((lines, n), 1), jnp.broadcast_to(coef, (lines, n)), 0.0),
+        axis=1, keepdims=True,
+    )
+
+    to_outer(recv_r, recv_r, send_sem.at[3], recv_sem.at[3], False)
 
     get_out.wait()
     settle(recv1, n - 1, recv_sem.at[0])
@@ -192,17 +203,26 @@
     total = recv_a[0].astype(F32)
     for i in range(1, inner):
         total += recv_a[i].astype(F32)
-    send_b[...] = total.reshape(outer, pieces, columns)
-    to_outer(send_b, recv_b, send_sem.at[2], recv_sem.at[2], True)
-    recv_b[a] = send_b[a]
+    recv_b[a] = total.astype(BF16)
+    to_outer(recv_b, recv_b, send_sem.at[2], recv_sem.at[2], False)
+    settle(recv_r, outer - 1, recv_sem.at[3])
     settle(recv_b, outer - 1, recv_sem.at[2])
-    hid = (rows2[0] + jnp.sum(recv_b[...], axis=0)).astype(BF16).astype(F32)
-    mean = jnp.sum(jnp.sum(hid * hid, axis=1, keepdims=True), axis=0, keepdims=True) / width
-    recv_c[a] = hid * lax.rsqrt(mean + 1e-06) * rows2[1]
-
-    to_outer(recv_c, recv_c, send_sem.at[3], recv_sem.at[3], False)
-    settle(recv_c, outer - 1, recv_sem.at[3])
-    recv_d[b] = recv_c[...].reshape(tile, columns).astype(BF16)
+    total = recv_b[0].astype(F32)
+    for i in range(1, outer):
+        total += recv_b[i].astype(F32)
+    hid = (recv_r[...].reshape(tile, columns) + total).astype(BF16).astype(F32)
+    hids[...] = hid.reshape(outer, pieces, columns)
+    squares = jnp.sum(hid * hid, axis=1, keepdims=True)
+    mates = iota((tile, tile), 0) // pieces == iota((tile, tile), 1) // pieces
+    mean = jnp.sum(
+        jnp.where(mates, jnp.broadcast_to(squares, (tile, tile)), 0.0), axis=0, keepdims=True
+    ) / width
+    mean = jnp.sum(
+        jnp.where(iota((tile, tile), 0) == iota((tile, tile), 1), jnp.broadcast_to(mean, (tile, tile)), 0.0),
+        axis=1, keepdims=True,
+    )
+
+    recv_d[b] = (hid * lax.rsqrt(mean + 1e-06) * gains[...]).astype(BF16)
     to_inner(recv_d, recv_d, send_sem.at[4], recv_sem.at[4], False)
     settle(recv_d, inner - 1, recv_sem.at[4])
     normed = recv_d[...].reshape(lines, columns)
@@ -242,17 +262,18 @@
         send_f[j] = total.reshape(outer, pieces, step)
         to_outer(send_f.at[j], recv_f.at[j], last_send.at[j], last_recv.at[j], True)
         recv_f[j, a] = send_f[j, a]
+    own = hids[a]
     for j in range(chunks):
         settle(recv_f.at[j], outer - 1, last_recv.at[j])
-        mixed = (hid[:, j * step : (j + 1) * step] + jnp.sum(recv_f[j], axis=0)).astype(BF16)
+        mixed = (own[:, j * step : (j + 1) * step] + jnp.sum(recv_f[j], axis=0)).astype(BF16)
         for p in range(pieces):
             start = p * columns + j * step
             out[:, start : start + step] = mixed[p : p + 1, :]
 
     settle(recv1, n - 1, send_sem.at[0])
     settle(send_a, inner - 1, send_sem.at[1])
-    settle(send_b, outer - 1, send_sem.at[2])
-    settle(recv_c, outer - 1, send_sem.at[3])
+    settle(recv_b, outer - 1, send_sem.at[2])
+    settle(recv_r, outer - 1, send_sem.at[3])
     settle(recv_d, inner - 1, send_sem.at[4])
     for j in range(chunks):
         settle(send_e.at[j], inner - 1, chunk_send.at[j])
@@ -270,35 +291,39 @@
     step = columns // chunks
     tile = outer * pieces
     hidden = w_gate.shape[1]
-    vmem = pl.BlockSpec(memory_space=pltpu.VMEM)
-    hbm = pl.BlockSpec(memory_space=pl.ANY)
+    hbm = pl.BlockSpec(memory_space=pltpu.HBM)
+    small = (
+        resid, query, key, value, decay.reshape(1, -1), out_gate, norm_gain.reshape(1, -1),
+        moe_gain.reshape(1, -1), expert_ids.T, expert_weights.T,
+    )
     sems = pltpu.SemaphoreType.DMA
     return pl.pallas_call(
         functools.partial(kernel, n, slab_split),
         out_shape=jax.ShapeDtypeStruct(resid.shape, resid.dtype),
-        in_specs=[vmem] * 10 + [hbm] * 5,
-        out_specs=vmem,
-        scratch_shapes=[
+        in_specs=[hbm] * 15,
+        out_specs=pl.BlockSpec(memory_space=pltpu.VMEM),
+        scratch_shapes=[pltpu.VMEM(x.shape, x.dtype) for x in small] + [
             pltpu.VMEM((heads * hdim, hdim), F32),
             pltpu.VMEM((hdim, width), BF16),
             pltpu.VMEM((hidden, width), BF16),
             pltpu.VMEM((hidden, width), BF16),
             pltpu.VMEM((hidden, width), BF16),
             pltpu.VMEM((5, heads, hdim), F32),
-            pltpu.VMEM((2, pieces, columns), F32),
+            pltpu.VMEM((tile, columns), F32),
+            pltpu.VMEM((outer, pieces, columns), F32),
             pltpu.VMEM((heads, 1, hdim), F32),
             pltpu.VMEM((n, 1, hdim), F32),
             pltpu.VMEM((inner, tile, columns), BF16),
             pltpu.VMEM((inner, tile, columns), BF16),
             pltpu.VMEM((outer, pieces, columns), F32),
-            pltpu.VMEM((outer, pieces, columns), F32),
-            pltpu.VMEM((outer, pieces, columns), F32),
+            pltpu.VMEM((outer, tile, columns), BF16),
             pltpu.VMEM((inner, tile, columns), BF16),
             pltpu.VMEM((pieces, n, columns), BF16),
             pltpu.VMEM((chunks, inner, tile, step), BF16),
             pltpu.VMEM((chunks, inner, tile, step), BF16),
             pltpu.VMEM((chunks, outer, pieces, step), F32),
             pltpu.VMEM((chunks, outer, pieces, step), F32),
+            sems((10,)),
             sems((STATE_CUTS + 4,)),
             sems((5,)),
             sems((5,)),
@@ -312,8 +337,7 @@
         ),
         name="decode_layer",
     )(
-        resid, query, key, value, decay.reshape(1, -1), out_gate, norm_gain.reshape(1, -1),
-        moe_gain.reshape(1, -1), expert_ids, expert_weights,
+        *small,
         state.reshape(heads * hdim, hdim), w_out, w_gate, w_up, w_down,
     )
 

time: 54.8 us -> 39.3 us (0.72)
  local copies, waits for them, and re-layouts: 14.5 us -> 1.32 us
  Pallas kernels: 39.5 us -> 37.7 us
    unnamed x27 -> x1, local copies, waits for them, and re-layouts: 14.5 us -> 1.32 us
    pallas_call x1, Pallas kernels: 39.5 us -> 37.7 us  [shards(): pl.pallas_call(functools.partial(kernel, n, slab_split), out_shape=jax.Sh...]
where the time goes in v2:
time: 39.3 us; the launch traced here: 39 us
  Pallas kernels  37.7 us (96%)
  local copies, waits for them, and re-layouts  1.32 us (3%)
    pallas_call x1, Pallas kernels, shards(): pl.pallas_call(functools.partial(kernel, n, slab_split), out_shape=jax.Sh...  37.7 us
    unnamed x1, local copies, waits for them, and re-layouts  1.32 us

profile of v2, /device:TPU:0, one launch (start us, length us, event | category | flops | bytes accessed | tf_op | source)
XLA Modules:
  0.0 39.0 jit_solution(736461120385137124)
XLA Ops:
  0.0 37.7 %decode_layer.1 = bf16[1,3072]{1,0:T(2,128)(2,1)} custom-call(bf16[1,3072]{1,0:T(2,128)(2,1)} %resid_h.1, bf16[1,4096]{1,0:T(2,128)(2,1)} %query_h.1, bf16[1,4096]{1,0:T(2,128)(2,1)} %key_h.1, bf16[1,4096]{1,0:T(2,128)(2,1)} %value_h.1, f32[1,32]{1,0:T(1,128)} %bitcast.11, bf16[1,4096]{1,0:T(2,128)(2,1)} %out_gate_h.1, f32[1,4096]{1,0:T(1,128)} %bitcast.7, ...), custom_call_target="tpu_custom_call" | custom-call | tf_op jit(solution)/shard_map/decode_layer/pallas_call | solution.py:300
  37.7 1.3 %copy.17 = bf16[1,3072]{1,0:T(2,128)(2,1)} copy(bf16[1,3072]{1,0:T(2,128)(2,1)} %decode_layer.1) | data formatting | bytes 12288

commit v3 on v2

--- a/solution.py
+++ b/solution.py
@@ -44,8 +44,8 @@
     resid, query, key, value, decay, out_gate, norm_gain, moe_gain, ids, weights,
     state, w_out, w_gate, w_up, w_down,
     heads5, gains, hids, att3, recv1, send_a, recv_a, recv_r, recv_b, recv_d,
-    xs, send_e, recv_e, send_f, recv_f,
-    small_sem, load_sem, send_sem, recv_sem, chunk_send, chunk_recv, last_send, last_recv,
+    recv_s, send_e, recv_e, send_f, recv_f,
+    small_sem, load_sem, send_sem, recv_sem, *sems,
 ):
     heads, hdim = att3.shape[0], att3.shape[2]
     width = resid.shape[1]
@@ -53,14 +53,14 @@
     step = columns // chunks
     share = w_out_h.shape[0]
     me = lax.axis_index("wide")
-    a, b = me // inner, me % inner
+    a, b = lax.div(me, inner), lax.rem(me, inner)
     tile = outer * pieces
 
     barrier = pltpu.get_barrier_semaphore()
 
     def greet(i, carry):
         pl.semaphore_signal(
-            barrier, inc=1, device_id={"wide": (me + i) % n},
+            barrier, inc=1, device_id={"wide": lax.rem(me + i, n)},
             device_id_type=pl.DeviceIdType.MESH,
         )
         return carry
@@ -132,45 +132,39 @@
 
     slot = b * outer + a
 
-    def send_head(i, carry):
-        peer = (me + i) % n
+    def head(device):
+        return device if share == hdim else lax.div(device * share, hdim)
+
+    for i in range(1, n):
+        peer = lax.rem(me + i, n)
         pltpu.make_async_remote_copy(
-            src_ref=att3.at[(peer * share) // hdim], dst_ref=recv1.at[slot],
+            src_ref=att3.at[head(peer)], dst_ref=recv1.at[slot],
             send_sem=send_sem.at[0], recv_sem=recv_sem.at[0],
             device_id={"wide": peer}, device_id_type=pl.DeviceIdType.MESH,
         ).start()
-        return carry
-
-    lax.fori_loop(1, n, send_head, 0)
-    recv1[slot] = att3[(me * share) // hdim]
+    recv1[slot] = att3[head(me)]
 
     def settle(ref, count, sem):
         view = ref.at[pl.ds(0, count)]
         pltpu.make_async_copy(view, view, sem).wait()
 
     def to_inner(src, dst, ssem, rsem, pick):
-        def one(i, carry):
-            peer = (b + i) % inner
+        for i in range(1, inner):
+            peer = lax.rem(b + i, inner)
             pltpu.make_async_remote_copy(
                 src_ref=src.at[peer if pick else b], dst_ref=dst.at[b],
                 send_sem=ssem, recv_sem=rsem,
                 device_id={"wide": a * inner + peer}, device_id_type=pl.DeviceIdType.MESH,
             ).start()
-            return carry
-
-        lax.fori_loop(1, inner, one, 0)
 
     def to_outer(src, dst, ssem, rsem, pick):
-        def one(i, carry):
-            peer = (a + i) % outer
+        for i in range(1, outer):
+            peer = lax.rem(a + i, outer)
             pltpu.make_async_remote_copy(
                 src_ref=src.at[peer if pick else a], dst_ref=dst.at[a],
                 send_sem=ssem, recv_sem=rsem,
                 device_id={"wide": peer * inner + b}, device_id_type=pl.DeviceIdType.MESH,
             ).start()
-            return carry
-
-        lax.fori_loop(1, outer, one, 0)
 
     lines = n * pieces
     spread = (iota((lines, n), 0) // pieces == iota((lines, n), 1)).astype(F32).astype(BF16)
@@ -188,61 +182,68 @@
         axis=1, keepdims=True,
     )
 
-    to_outer(recv_r, recv_r, send_sem.at[3], recv_sem.at[3], False)
+    to_outer(recv_r, recv_r, send_sem.at[1], recv_sem.at[1], False)
 
     get_out.wait()
     settle(recv1, n - 1, recv_sem.at[0])
     full = dot(spread, recv1[...].reshape(n, hdim).astype(BF16))
-    proj = jnp.zeros((lines, columns), F32)
-    for p in range(pieces):
-        proj += dot(only(p, full), w_out[:, p * columns : (p + 1) * columns])
-    send_a[...] = proj.astype(BF16).reshape(inner, tile, columns)
-    to_inner(send_a, recv_a, send_sem.at[1], recv_sem.at[1], True)
-    recv_a[b] = send_a[b]
-    settle(recv_a, inner - 1, recv_sem.at[1])
-    total = recv_a[0].astype(F32)
-    for i in range(1, inner):
-        total += recv_a[i].astype(F32)
-    recv_b[a] = total.astype(BF16)
-    to_outer(recv_b, recv_b, send_sem.at[2], recv_sem.at[2], False)
-    settle(recv_r, outer - 1, recv_sem.at[3])
-    settle(recv_b, outer - 1, recv_sem.at[2])
-    total = recv_b[0].astype(F32)
-    for i in range(1, outer):
-        total += recv_b[i].astype(F32)
-    hid = (recv_r[...].reshape(tile, columns) + total).astype(BF16).astype(F32)
-    hids[...] = hid.reshape(outer, pieces, columns)
-    squares = jnp.sum(hid * hid, axis=1, keepdims=True)
-    mates = iota((tile, tile), 0) // pieces == iota((tile, tile), 1) // pieces
+    for c in range(chunks):
+        proj = jnp.zeros((lines, step), F32)
+        for p in range(pieces):
+            start = p * columns + c * step
+            proj += dot(only(p, full), w_out[:, start : start + step])
+        send_a[c] = proj.astype(BF16).reshape(inner, tile, step)
+        to_inner(send_a.at[c], recv_a.at[c], sems[0].at[c], sems[1].at[c], True)
+        recv_a[c, b] = send_a[c, b]
+    for c in range(chunks):
+        settle(recv_a.at[c], inner - 1, sems[1].at[c])
+        total = recv_a[c, 0].astype(F32)
+        for i in range(1, inner):
+            total += recv_a[c, i].astype(F32)
+        recv_b[c, a] = total.astype(BF16)
+        to_outer(recv_b.at[c], recv_b.at[c], sems[2].at[c], sems[3].at[c], False)
+    settle(recv_r, outer - 1, recv_sem.at[1])
+    squares = jnp.zeros((tile, 1), F32)
+    for c in range(chunks):
+        settle(recv_b.at[c], outer - 1, sems[3].at[c])
+        total = recv_b[c, 0].astype(F32)
+        for i in range(1, outer):
+            total += recv_b[c, i].astype(F32)
+        at = slice(c * step, (c + 1) * step)
+        hid = (recv_r[:, :, at].reshape(tile, step) + total).astype(BF16).astype(F32)
+        recv_d[c, b] = (hid * gains[:, at]).astype(BF16)
+        to_inner(recv_d.at[c], recv_d.at[c], sems[4].at[c], sems[5].at[c], False)
+        hids[c] = hid.reshape(outer, pieces, step)
+        squares += jnp.sum(hid * hid, axis=1, keepdims=True)
+    mates = iota((tile, outer), 0) // pieces == iota((tile, outer), 1)
     mean = jnp.sum(
-        jnp.where(mates, jnp.broadcast_to(squares, (tile, tile)), 0.0), axis=0, keepdims=True
+        jnp.where(mates, jnp.broadcast_to(squares, (tile, outer)), 0.0), axis=0, keepdims=True
     ) / width
-    mean = jnp.sum(
-        jnp.where(iota((tile, tile), 0) == iota((tile, tile), 1), jnp.broadcast_to(mean, (tile, tile)), 0.0),
+    same = iota((outer, outer), 0) == iota((outer, outer), 1)
+    scale = jnp.sum(
+        jnp.where(same, jnp.broadcast_to(lax.rsqrt(mean + 1e-06), (outer, outer)), 0.0),
         axis=1, keepdims=True,
     )
-
-    recv_d[b] = (hid * lax.rsqrt(mean + 1e-06) * gains[...]).astype(BF16)
-    to_inner(recv_d, recv_d, send_sem.at[4], recv_sem.at[4], False)
-    settle(recv_d, inner - 1, recv_sem.at[4])
-    normed = recv_d[...].reshape(lines, columns)
-    at_line = iota((n, lines), 0) * pieces
-    for p in range(pieces):
-        pick = (iota((n, lines), 1) == at_line + p).astype(F32).astype(BF16)
-        xs[p] = dot(pick, normed).astype(BF16)
+    recv_s[b] = jnp.broadcast_to(scale, (outer, hdim)).reshape(outer, 1, hdim)
+    to_inner(recv_s, recv_s, send_sem.at[2], recv_sem.at[2], False)
 
     big[0].wait()
     big[1].wait()
     hidden = w_gate.shape[0]
-
-    def piece(p, carry):
-        gate, upper = carry
-        at = pl.ds(pl.multiple_of(p * columns, columns), columns)
-        x = xs[p]
-        return gate + by_rows(x, w_gate[:, at]), upper + by_rows(x, w_up[:, at])
-
-    zero = jnp.zeros((n, hidden), F32)
-    gate, upper = lax.fori_loop(0, pieces, piece, (zero, zero))
+    gate, upper = jnp.zeros((n, hidden), F32), jnp.zeros((n, hidden), F32)
+    at_line = iota((n, lines), 0) * pieces
+    for c in range(chunks):
+        settle(recv_d.at[c], inner - 1, sems[5].at[c])
+        part = recv_d[c].reshape(lines, step)
+        for p in range(pieces):
+            pick = (iota((n, lines), 1) == at_line + p).astype(F32).astype(BF16)
+            x = dot(pick, part).astype(BF16)
+            start = p * columns + c * step
+            gate += by_rows(x, w_gate[:, start : start + step])
+            upper += by_rows(x, w_up[:, start : start + step])
+    settle(recv_s, inner - 1, recv_sem.at[2])
+    scale = recv_s[...].reshape(n, hdim)[:, :1]
+    gate, upper = gate * scale, upper * scale
     inner_act = (gate * jax.nn.sigmoid(gate) * upper).astype(BF16)
     full = dot(spread, inner_act)
     big[2].wait()
@@ -252,32 +253,32 @@
             start = p * columns + j * step
             acc += dot(only(p, full), w_down[:, start : start + step])
         send_e[j] = (acc * coef_line).astype(BF16).reshape(inner, tile, step)
-        to_inner(send_e.at[j], recv_e.at[j], chunk_send.at[j], chunk_recv.at[j], True)
+        to_inner(send_e.at[j], recv_e.at[j], sems[6].at[j], sems[7].at[j], True)
         recv_e[j, b] = send_e[j, b]
     for j in range(chunks):
-        settle(recv_e.at[j], inner - 1, chunk_recv.at[j])
+        settle(recv_e.at[j], inner - 1, sems[7].at[j])
         total = recv_e[j, 0].astype(F32)
         for i in range(1, inner):
             total += recv_e[j, i].astype(F32)
         send_f[j] = total.reshape(outer, pieces, step)
-        to_outer(send_f.at[j], recv_f.at[j], last_send.at[j], last_recv.at[j], True)
+        to_outer(send_f.at[j], recv_f.at[j], sems[8].at[j], sems[9].at[j], True)
         recv_f[j, a] = send_f[j, a]
-    own = hids[a]
     for j in range(chunks):
-        settle(recv_f.at[j], outer - 1, last_recv.at[j])
-        mixed = (own[:, j * step : (j + 1) * step] + jnp.sum(recv_f[j], axis=0)).astype(BF16)
+        settle(recv_f.at[j], outer - 1, sems[9].at[j])
+        mixed = (hids[j, a] + jnp.sum(recv_f[j], axis=0)).astype(BF16)
         for p in range(pieces):
             start = p * columns + j * step
             out[:, start : start + step] = mixed[p : p + 1, :]
 
     settle(recv1, n - 1, send_sem.at[0])
-    settle(send_a, inner - 1, send_sem.at[1])
-    settle(recv_b, outer - 1, send_sem.at[2])
-    settle(recv_r, outer - 1, send_sem.at[3])
-    settle(recv_d, inner - 1, send_sem.at[4])
+    settle(recv_r, outer - 1, send_sem.at[1])
+    settle(recv_s, inner - 1, send_sem.at[2])
     for j in range(chunks):
-        settle(send_e.at[j], inner - 1, chunk_send.at[j])
-        settle(send_f.at[j], outer - 1, last_send.at[j])
+        settle(send_a.at[j], inner - 1, sems[0].at[j])
+        settle(recv_b.at[j], outer - 1, sems[2].at[j])
+        settle(recv_d.at[j], inner - 1, sems[4].at[j])
+        settle(send_e.at[j], inner - 1, sems[6].at[j])
+        settle(send_f.at[j], outer - 1, sems[8].at[j])
 
 
 def shards(
@@ -310,28 +311,24 @@
             pltpu.VMEM((hidden, width), BF16),
             pltpu.VMEM((5, heads, hdim), F32),
             pltpu.VMEM((tile, columns), F32),
-            pltpu.VMEM((outer, pieces, columns), F32),
+            pltpu.VMEM((chunks, outer, pieces, step), F32),
             pltpu.VMEM((heads, 1, hdim), F32),
             pltpu.VMEM((n, 1, hdim), F32),
-            pltpu.VMEM((inner, tile, columns), BF16),
-            pltpu.VMEM((inner, tile, columns), BF16),
+            pltpu.VMEM((chunks, inner, tile, step), BF16),
+            pltpu.VMEM((chunks, inner, tile, step), BF16),
             pltpu.VMEM((outer, pieces, columns), F32),
-            pltpu.VMEM((outer, tile, columns), BF16),
-            pltpu.VMEM((inner, tile, columns), BF16),
-            pltpu.VMEM((pieces, n, columns), BF16),
+            pltpu.VMEM((chunks, outer, tile, step), BF16),
+            pltpu.VMEM((chunks, inner, tile, step), BF16),
+            pltpu.VMEM((inner, outer, 1, hdim), F32),
             pltpu.VMEM((chunks, inner, tile, step), BF16),
             pltpu.VMEM((chunks, inner, tile, step), BF16),
             pltpu.VMEM((chunks, outer, pieces, step), F32),
             pltpu.VMEM((chunks, outer, pieces, step), F32),
             sems((10,)),
             sems((STATE_CUTS + 4,)),
-            sems((5,)),
-            sems((5,)),
-            sems((chunks,)),
-            sems((chunks,)),
-            sems((chunks,)),
-            sems((chunks,)),
-        ],
+            sems((3,)),
+            sems((3,)),
+        ] + [sems((chunks,))] * 10,
         compiler_params=pltpu.CompilerParams(
             collective_id=0, has_side_effects=True, vmem_limit_bytes=VMEM
         ),

time: 39.3 us -> 38 us (0.967)
  Pallas kernels: 37.7 us -> 36.3 us
    pallas_call x1, Pallas kernels: 37.7 us -> 36.3 us  [shards(): pl.pallas_call(functools.partial(kernel, n, slab_split), out_shape=jax.Sh...]
where the time goes in v3:
time: 38 us; the launch traced here: 37.7 us
  Pallas kernels  36.3 us (96%)
  local copies, waits for them, and re-layouts  1.32 us (3%)
    pallas_call x1, Pallas kernels, shards(): pl.pallas_call(functools.partial(kernel, n, slab_split), out_shape=jax.Sh...  36.3 us
    unnamed x1, local copies, waits for them, and re-layouts  1.32 us

profile of v3, /device:TPU:0, one launch (start us, length us, event | category | flops | bytes accessed | tf_op | source)
XLA Modules:
  0.0 37.7 jit_solution(2536558128451293834)
XLA Ops:
  0.0 36.3 %decode_layer.1 = bf16[1,3072]{1,0:T(2,128)(2,1)} custom-call(bf16[1,3072]{1,0:T(2,128)(2,1)} %resid_h.1, bf16[1,4096]{1,0:T(2,128)(2,1)} %query_h.1, bf16[1,4096]{1,0:T(2,128)(2,1)} %key_h.1, bf16[1,4096]{1,0:T(2,128)(2,1)} %value_h.1, f32[1,32]{1,0:T(1,128)} %bitcast.11, bf16[1,4096]{1,0:T(2,128)(2,1)} %out_gate_h.1, f32[1,4096]{1,0:T(1,128)} %bitcast.7, ...), custom_call_target="tpu_custom_call" | custom-call | tf_op jit(solution)/shard_map/decode_layer/pallas_call | solution.py:301
  36.4 1.3 %copy.17 = bf16[1,3072]{1,0:T(2,128)(2,1)} copy(bf16[1,3072]{1,0:T(2,128)(2,1)} %decode_layer.1) | data formatting | bytes 12288

commit v4 on v3

--- a/solution.py
+++ b/solution.py
@@ -86,25 +86,14 @@
         place = pl.ds(pl.multiple_of((me * share) % hdim, share), share)
         get_out = pltpu.make_async_copy(w_out_h, w_out.at[place], load_sem.at[STATE_CUTS])
     get_out.start()
-    big = []
-    for i, (src, dst) in enumerate(((w_gate_h, w_gate), (w_up_h, w_up), (w_down_h, w_down))):
-        big.append(pltpu.make_async_copy(src.at[0], dst, load_sem.at[STATE_CUTS + 1 + i]))
-        big[-1].start()
-
     lax.fori_loop(1, n, greet, 0)
 
-    for copy in small:
+    for copy in small[:6]:
         copy.wait()
     for i, ref in enumerate((query, key, value, out_gate, norm_gain)):
         line = ref[...].astype(F32)
         for h in range(heads):
             heads5[i, h : h + 1, :] = line[:, h * hdim : (h + 1) * hdim]
-    line = resid[...].astype(F32)
-    for p in range(pieces):
-        recv_r[a, p : p + 1, :] = line[:, p * columns : (p + 1) * columns]
-        for i in range(outer):
-            at = i * pieces + p
-            gains[at : at + 1, :] = moe_gain[:, p * columns : (p + 1) * columns]
     q, k, v = heads5[0], heads5[1], heads5[2]
     head_of = iota((heads, hdim), 0)
     eye = iota((heads, heads), 0) == iota((heads, heads), 1)
@@ -144,6 +133,11 @@
         ).start()
     recv1[slot] = att3[head(me)]
 
+    big = []
+    for i, (src, dst) in enumerate(((w_gate_h, w_gate), (w_up_h, w_up), (w_down_h, w_down))):
+        big.append(pltpu.make_async_copy(src.at[0], dst, load_sem.at[STATE_CUTS + 1 + i]))
+        big[-1].start()
+
     def settle(ref, count, sem):
         view = ref.at[pl.ds(0, count)]
         pltpu.make_async_copy(view, view, sem).wait()
@@ -166,6 +160,9 @@
                 device_id={"wide": peer * inner + b}, device_id_type=pl.DeviceIdType.MESH,
             ).start()
 
+    for copy in small[6:]:
+        copy.wait()
+
     lines = n * pieces
     spread = (iota((lines, n), 0) // pieces == iota((lines, n), 1)).astype(F32).astype(BF16)
     piece_of = iota((lines, 1), 0) % pieces
@@ -182,6 +179,12 @@
         axis=1, keepdims=True,
     )
 
+    line = resid[...].astype(F32)
+    for p in range(pieces):
+        recv_r[a, p : p + 1, :] = line[:, p * columns : (p + 1) * columns]
+        for i in range(outer):
+            at = i * pieces + p
+            gains[at : at + 1, :] = moe_gain[:, p * columns : (p + 1) * columns]
     to_outer(recv_r, recv_r, send_sem.at[1], recv_sem.at[1], False)
 
     get_out.wait()
@@ -300,7 +303,7 @@
     sems = pltpu.SemaphoreType.DMA
     return pl.pallas_call(
         functools.partial(kernel, n, slab_split),
-        out_shape=jax.ShapeDtypeStruct(resid.shape, resid.dtype),
+        out_shape=pltpu.VMEM(resid.shape, resid.dtype),
         in_specs=[hbm] * 15,
         out_specs=pl.BlockSpec(memory_space=pltpu.VMEM),
         scratch_shapes=[pltpu.VMEM(x.shape, x.dtype) for x in small] + [

time: 38 us -> 34.2 us (0.900)
  Pallas kernels: 36.3 us -> 33.4 us
  local copies, waits for them, and re-layouts: 1.32 us -> 0.6 us
    pallas_call x1, Pallas kernels: 36.3 us -> 33.4 us  [shards(): pl.pallas_call(functools.partial(kernel, n, slab_split), out_shape=pltpu....]
    unnamed x1, local copies, waits for them, and re-layouts: 1.32 us -> 0.6 us
where the time goes in v4:
time: 34.2 us; the launch traced here: 34 us
  Pallas kernels  33.4 us (98%)
  local copies, waits for them, and re-layouts  0.6 us (2%)
    pallas_call x1, Pallas kernels, shards(): pl.pallas_call(functools.partial(kernel, n, slab_split), out_shape=pltpu....  33.4 us

profile of v4, /device:TPU:0, one launch (start us, length us, event | category | flops | bytes accessed | tf_op | source)
XLA Modules:
  0.0 34.0 jit_solution(10248471542799388523)
XLA Ops:
  0.0 33.4 %decode_layer.1 = bf16[1,3072]{1,0:T(2,128)(2,1)S(1)} custom-call(bf16[1,3072]{1,0:T(2,128)(2,1)} %resid_h.1, bf16[1,4096]{1,0:T(2,128)(2,1)} %query_h.1, bf16[1,4096]{1,0:T(2,128)(2,1)} %key_h.1, bf16[1,4096]{1,0:T(2,128)(2,1)} %value_h.1, f32[1,32]{1,0:T(1,128)} %bitcast.11, bf16[1,4096]{1,0:T(2,128)(2,1)} %out_gate_h.1, f32[1,4096]{1,0:T(1,128)} %bitcast.7, ...), custom_call_target="tpu_custom_call" | custom-call | tf_op jit(solution)/shard_map/decode_layer/pallas_call | solution.py:304
  33.4 0.6 %copy.17 = bf16[1,3072]{1,0:T(2,128)(2,1)} copy(bf16[1,3072]{1,0:T(2,128)(2,1)S(1)} %decode_layer.1) | data formatting | bytes 12288

commit v5 on v4

--- a/solution.py
+++ b/solution.py
@@ -95,48 +95,53 @@
         for h in range(heads):
             heads5[i, h : h + 1, :] = line[:, h * hdim : (h + 1) * hdim]
     q, k, v = heads5[0], heads5[1], heads5[2]
-    head_of = iota((heads, hdim), 0)
     eye = iota((heads, heads), 0) == iota((heads, heads), 1)
     fade = jnp.sum(
         jnp.where(eye, jnp.broadcast_to(jnp.exp(-decay[...]), (heads, heads)), 0.0),
         axis=1, keepdims=True,
     )
-    att = jnp.zeros((heads, hdim), F32)
-    per_cut = heads // STATE_CUTS
-    for c in range(STATE_CUTS):
-        diagonal = jnp.concatenate(
-            [jnp.where(head_of == c * per_cut + h, q, 0.0).astype(BF16) for h in range(per_cut)],
-            axis=1,
-        )
-        loads[c].wait()
-        att += dot(diagonal, state[pl.ds(c * part, part), :].astype(BF16))
-    att = fade * att + jnp.sum(q * k, axis=1, keepdims=True) * v
-    mean = jnp.sum(jnp.sum(att * att, axis=1, keepdims=True), axis=0, keepdims=True) / (
-        heads * hdim
-    )
-    attn = att * lax.rsqrt(mean + 1e-06) * heads5[4] * jax.nn.sigmoid(heads5[3])
-    att3[...] = attn.reshape(heads, 1, hdim)
-
-    pl.semaphore_wait(barrier, n - 1)
-
     slot = b * outer + a
 
     def head(device):
         return device if share == hdim else lax.div(device * share, hdim)
 
-    for i in range(1, n):
-        peer = lax.rem(me + i, n)
+    def send_head(peer):
         pltpu.make_async_remote_copy(
             src_ref=att3.at[head(peer)], dst_ref=recv1.at[slot],
             send_sem=send_sem.at[0], recv_sem=recv_sem.at[0],
             device_id={"wide": peer}, device_id_type=pl.DeviceIdType.MESH,
         ).start()
+
+    per_cut, holders = heads // STATE_CUTS, n // STATE_CUTS
+    squares = jnp.zeros((per_cut, 1), F32)
+    for c in range(STATE_CUTS):
+        at = slice(c * per_cut, (c + 1) * per_cut)
+        q_c = q[at]
+        row = iota((per_cut, hdim), 0)
+        diagonal = jnp.concatenate(
+            [jnp.where(row == h, q_c, 0.0) for h in range(per_cut)], axis=1
+        ).astype(BF16)
+        loads[c].wait()
+        att = dot(diagonal, state[pl.ds(c * part, part), :].astype(BF16))
+        att = fade[at] * att + jnp.sum(q_c * k[at], axis=1, keepdims=True) * v[at]
+        squares += jnp.sum(att * att, axis=1, keepdims=True)
+        attn = att * heads5[4, at, :] * jax.nn.sigmoid(heads5[3, at, :])
+        att3[at] = attn.reshape(per_cut, 1, hdim)
+        if c == 0:
+            pl.semaphore_wait(barrier, n - 1)
+        first = c * holders + lax.rem(me, holders)
+        pl.when(first != me)(functools.partial(send_head, first))
+        for i in range(1, holders):
+            send_head(c * holders + lax.rem(me + i, holders))
     recv1[slot] = att3[head(me)]
+    mean = jnp.sum(squares, axis=0, keepdims=True) / (heads * hdim)
+    scale = lax.rsqrt(mean + 1e-06)
 
     big = []
     for i, (src, dst) in enumerate(((w_gate_h, w_gate), (w_up_h, w_up), (w_down_h, w_down))):
         big.append(pltpu.make_async_copy(src.at[0], dst, load_sem.at[STATE_CUTS + 1 + i]))
-        big[-1].start()
+
+    big[0].start()
 
     def settle(ref, count, sem):
         view = ref.at[pl.ds(0, count)]
@@ -179,6 +184,7 @@
         axis=1, keepdims=True,
     )
 
+    recv_r[a, pieces : pieces + 1, :] = jnp.broadcast_to(scale, (1, columns))
     line = resid[...].astype(F32)
     for p in range(pieces):
         recv_r[a, p : p + 1, :] = line[:, p * columns : (p + 1) * columns]
@@ -198,6 +204,7 @@
         send_a[c] = proj.astype(BF16).reshape(inner, tile, step)
         to_inner(send_a.at[c], recv_a.at[c], sems[0].at[c], sems[1].at[c], True)
         recv_a[c, b] = send_a[c, b]
+    big[1].start()
     for c in range(chunks):
         settle(recv_a.at[c], inner - 1, sems[1].at[c])
         total = recv_a[c, 0].astype(F32)
@@ -205,7 +212,11 @@
             total += recv_a[c, i].astype(F32)
         recv_b[c, a] = total.astype(BF16)
         to_outer(recv_b.at[c], recv_b.at[c], sems[2].at[c], sems[3].at[c], False)
+    big[2].start()
     settle(recv_r, outer - 1, recv_sem.at[1])
+    scale = jnp.broadcast_to(
+        recv_r[:, pieces : pieces + 1, :step], (outer, pieces, step)
+    ).reshape(tile, step)
     squares = jnp.zeros((tile, 1), F32)
     for c in range(chunks):
         settle(recv_b.at[c], outer - 1, sems[3].at[c])
@@ -213,7 +224,7 @@
         for i in range(1, outer):
             total += recv_b[c, i].astype(F32)
         at = slice(c * step, (c + 1) * step)
-        hid = (recv_r[:, :, at].reshape(tile, step) + total).astype(BF16).astype(F32)
+        hid = (recv_r[:, :pieces, at].reshape(tile, step) + total * scale).astype(BF16).astype(F32)
         recv_d[c, b] = (hid * gains[:, at]).astype(BF16)
         to_inner(recv_d.at[c], recv_d.at[c], sems[4].at[c], sems[5].at[c], False)
         hids[c] = hid.reshape(outer, pieces, step)
@@ -319,7 +330,7 @@
             pltpu.VMEM((n, 1, hdim), F32),
             pltpu.VMEM((chunks, inner, tile, step), BF16),
             pltpu.VMEM((chunks, inner, tile, step), BF16),
-            pltpu.VMEM((outer, pieces, columns), F32),
+            pltpu.VMEM((outer, pieces + 1, columns), F32),
             pltpu.VMEM((chunks, outer, tile, step), BF16),
             pltpu.VMEM((chunks, inner, tile, step), BF16),
             pltpu.VMEM((inner, outer, 1, hdim), F32),

time: 34.2 us -> 34.6 us (1.012)
  no operation moved by 1% of the time
where the time goes in v5:
time: 34.6 us; the launch traced here: 34.4 us
  Pallas kernels  33.7 us (97%)
  local copies, waits for them, and re-layouts  0.6 us (2%)
    pallas_call x1, Pallas kernels, shards(): pl.pallas_call(functools.partial(kernel, n, slab_split), out_shape=pltpu....  33.7 us

profile of v5, /device:TPU:0, one launch (start us, length us, event | category | flops | bytes accessed | tf_op | source)
XLA Modules:
  0.0 34.4 jit_solution(10133491610415679758)
XLA Ops:
  0.0 33.7 %decode_layer.1 = bf16[1,3072]{1,0:T(2,128)(2,1)S(1)} custom-call(bf16[1,3072]{1,0:T(2,128)(2,1)} %resid_h.1, bf16[1,4096]{1,0:T(2,128)(2,1)} %query_h.1, bf16[1,4096]{1,0:T(2,128)(2,1)} %key_h.1, bf16[1,4096]{1,0:T(2,128)(2,1)} %value_h.1, f32[1,32]{1,0:T(1,128)} %bitcast.11, bf16[1,4096]{1,0:T(2,128)(2,1)} %out_gate_h.1, f32[1,4096]{1,0:T(1,128)} %bitcast.7, ...), custom_call_target="tpu_custom_call" | custom-call | tf_op jit(solution)/shard_map/decode_layer/pallas_call | solution.py:315
  33.8 0.6 %copy.17 = bf16[1,3072]{1,0:T(2,128)(2,1)} copy(bf16[1,3072]{1,0:T(2,128)(2,1)S(1)} %decode_layer.1) | data formatting | bytes 12288

commit v6 on v4

--- a/solution.py
+++ b/solution.py
@@ -95,21 +95,22 @@
         for h in range(heads):
             heads5[i, h : h + 1, :] = line[:, h * hdim : (h + 1) * hdim]
     q, k, v = heads5[0], heads5[1], heads5[2]
-    head_of = iota((heads, hdim), 0)
     eye = iota((heads, heads), 0) == iota((heads, heads), 1)
     fade = jnp.sum(
         jnp.where(eye, jnp.broadcast_to(jnp.exp(-decay[...]), (heads, heads)), 0.0),
         axis=1, keepdims=True,
     )
-    att = jnp.zeros((heads, hdim), F32)
     per_cut = heads // STATE_CUTS
+    row = iota((per_cut, hdim), 0)
+    cuts = []
     for c in range(STATE_CUTS):
+        q_c = q[c * per_cut : (c + 1) * per_cut]
         diagonal = jnp.concatenate(
-            [jnp.where(head_of == c * per_cut + h, q, 0.0).astype(BF16) for h in range(per_cut)],
-            axis=1,
-        )
+            [jnp.where(row == h, q_c, 0.0) for h in range(per_cut)], axis=1
+        ).astype(BF16)
         loads[c].wait()
-        att += dot(diagonal, state[pl.ds(c * part, part), :].astype(BF16))
+        cuts.append(dot(diagonal, state[pl.ds(c * part, part), :].astype(BF16)))
+    att = jnp.concatenate(cuts, axis=0)
     att = fade * att + jnp.sum(q * k, axis=1, keepdims=True) * v
     mean = jnp.sum(jnp.sum(att * att, axis=1, keepdims=True), axis=0, keepdims=True) / (
         heads * hdim
@@ -172,10 +173,10 @@
 
     owner = me // slab_split
     coef = jnp.sum(jnp.where(ids[...] == owner, weights[...], 0.0), axis=0, keepdims=True)
-    line = iota((lines, n), 0) // pieces
-    request = (line % outer) * inner + line // outer
-    coef_line = jnp.sum(
-        jnp.where(request == iota((lines, n), 1), jnp.broadcast_to(coef, (lines, n)), 0.0),
+    line = iota((n, n), 0)
+    request = lax.rem(line, outer) * inner + lax.div(line, outer)
+    coef = jnp.sum(
+        jnp.where(request == iota((n, n), 1), jnp.broadcast_to(coef, (n, n)), 0.0),
         axis=1, keepdims=True,
     )
 
@@ -234,13 +235,17 @@
     big[1].wait()
     hidden = w_gate.shape[0]
     gate, upper = jnp.zeros((n, hidden), F32), jnp.zeros((n, hidden), F32)
-    at_line = iota((n, lines), 0) * pieces
+    to = iota((lines, lines), 0)
+    sort = (iota((lines, lines), 1) == lax.rem(to, n) * pieces + lax.div(to, n)).astype(F32)
+    sort = sort.astype(BF16)
+    unsort = (iota((lines, lines), 1) == lax.rem(to, pieces) * n + lax.div(to, pieces)).astype(F32)
+    unsort = unsort.astype(BF16)
     for c in range(chunks):
         settle(recv_d.at[c], inner - 1, sems[5].at[c])
         part = recv_d[c].reshape(lines, step)
+        every = dot(sort, part).astype(BF16)
         for p in range(pieces):
-            pick = (iota((n, lines), 1) == at_line + p).astype(F32).astype(BF16)
-            x = dot(pick, part).astype(BF16)
+            x = every[p * n : (p + 1) * n]
             start = p * columns + c * step
             gate += by_rows(x, w_gate[:, start : start + step])
             upper += by_rows(x, w_up[:, start : start + step])
@@ -248,14 +253,14 @@
     scale = recv_s[...].reshape(n, hdim)[:, :1]
     gate, upper = gate * scale, upper * scale
     inner_act = (gate * jax.nn.sigmoid(gate) * upper).astype(BF16)
-    full = dot(spread, inner_act)
     big[2].wait()
     for j in range(chunks):
-        acc = jnp.zeros((lines, step), F32)
+        lot = []
         for p in range(pieces):
             start = p * columns + j * step
-            acc += dot(only(p, full), w_down[:, start : start + step])
-        send_e[j] = (acc * coef_line).astype(BF16).reshape(inner, tile, step)
+            lot.append((dot(inner_act, w_down[:, start : start + step]) * coef).astype(BF16))
+        lot = dot(unsort, jnp.concatenate(lot, axis=0))
+        send_e[j] = lot.astype(BF16).reshape(inner, tile, step)
         to_inner(send_e.at[j], recv_e.at[j], sems[6].at[j], sems[7].at[j], True)
         recv_e[j, b] = send_e[j, b]
     for j in range(chunks):

time: 34.2 us -> 33.6 us (0.982)
  Pallas kernels: 33.4 us -> 32.8 us
    pallas_call x1, Pallas kernels: 33.4 us -> 32.8 us  [shards(): pl.pallas_call(functools.partial(kernel, n, slab_split), out_shape=pltpu....]
where the time goes in v6:
time: 33.6 us; the launch traced here: 33.4 us
  Pallas kernels  32.8 us (98%)
  local copies, waits for them, and re-layouts  0.6 us (2%)
    pallas_call x1, Pallas kernels, shards(): pl.pallas_call(functools.partial(kernel, n, slab_split), out_shape=pltpu....  32.8 us

profile of v6, /device:TPU:0, one launch (start us, length us, event | category | flops | bytes accessed | tf_op | source)
XLA Modules:
  0.0 33.4 jit_solution(8589019254493384022)
XLA Ops:
  0.0 32.8 %decode_layer.1 = bf16[1,3072]{1,0:T(2,128)(2,1)S(1)} custom-call(bf16[1,3072]{1,0:T(2,128)(2,1)} %resid_h.1, bf16[1,4096]{1,0:T(2,128)(2,1)} %query_h.1, bf16[1,4096]{1,0:T(2,128)(2,1)} %key_h.1, bf16[1,4096]{1,0:T(2,128)(2,1)} %value_h.1, f32[1,32]{1,0:T(1,128)} %bitcast.11, bf16[1,4096]{1,0:T(2,128)(2,1)} %out_gate_h.1, f32[1,4096]{1,0:T(1,128)} %bitcast.7, ...), custom_call_target="tpu_custom_call" | custom-call | tf_op jit(solution)/shard_map/decode_layer/pallas_call | solution.py:309
  32.8 0.6 %copy.17 = bf16[1,3072]{1,0:T(2,128)(2,1)} copy(bf16[1,3072]{1,0:T(2,128)(2,1)S(1)} %decode_layer.1) | data formatting | bytes 12288

commit v7 on v6

--- a/solution.py
+++ b/solution.py
@@ -165,11 +165,11 @@
         copy.wait()
 
     lines = n * pieces
-    spread = (iota((lines, n), 0) // pieces == iota((lines, n), 1)).astype(F32).astype(BF16)
-    piece_of = iota((lines, 1), 0) % pieces
-
-    def only(p, full):
-        return jnp.where(piece_of == p, full, 0.0).astype(BF16)
+    to = iota((lines, lines), 0)
+    sort = (iota((lines, lines), 1) == lax.rem(to, n) * pieces + lax.div(to, n)).astype(F32)
+    sort = sort.astype(BF16)
+    unsort = (iota((lines, lines), 1) == lax.rem(to, pieces) * n + lax.div(to, pieces)).astype(F32)
+    unsort = unsort.astype(BF16)
 
     owner = me // slab_split
     coef = jnp.sum(jnp.where(ids[...] == owner, weights[...], 0.0), axis=0, keepdims=True)
@@ -190,13 +190,14 @@
 
     get_out.wait()
     settle(recv1, n - 1, recv_sem.at[0])
-    full = dot(spread, recv1[...].reshape(n, hdim).astype(BF16))
+    features = recv1[...].reshape(n, hdim).astype(BF16)
     for c in range(chunks):
-        proj = jnp.zeros((lines, step), F32)
+        lot = []
         for p in range(pieces):
             start = p * columns + c * step
-            proj += dot(only(p, full), w_out[:, start : start + step])
-        send_a[c] = proj.astype(BF16).reshape(inner, tile, step)
+            lot.append(dot(features, w_out[:, start : start + step]).astype(BF16))
+        lot = dot(unsort, jnp.concatenate(lot, axis=0))
+        send_a[c] = lot.astype(BF16).reshape(inner, tile, step)
         to_inner(send_a.at[c], recv_a.at[c], sems[0].at[c], sems[1].at[c], True)
         recv_a[c, b] = send_a[c, b]
     for c in range(chunks):
@@ -235,11 +236,6 @@
     big[1].wait()
     hidden = w_gate.shape[0]
     gate, upper = jnp.zeros((n, hidden), F32), jnp.zeros((n, hidden), F32)
-    to = iota((lines, lines), 0)
-    sort = (iota((lines, lines), 1) == lax.rem(to, n) * pieces + lax.div(to, n)).astype(F32)
-    sort = sort.astype(BF16)
-    unsort = (iota((lines, lines), 1) == lax.rem(to, pieces) * n + lax.div(to, pieces)).astype(F32)
-    unsort = unsort.astype(BF16)
     for c in range(chunks):
         settle(recv_d.at[c], inner - 1, sems[5].at[c])
         part = recv_d[c].reshape(lines, step)

time: 33.6 us -> 33.3 us (level)
  no operation moved by 1% of the time
where the time goes in v7:
time: 33.3 us; the launch traced here: 33.1 us
  Pallas kernels  32.5 us (98%)
  local copies, waits for them, and re-layouts  0.6 us (2%)
    pallas_call x1, Pallas kernels, shards(): pl.pallas_call(functools.partial(kernel, n, slab_split), out_shape=pltpu....  32.5 us

profile of v7, /device:TPU:0, one launch (start us, length us, event | category | flops | bytes accessed | tf_op | source)
XLA Modules:
  0.0 33.1 jit_solution(6768408588273030107)
XLA Ops:
  0.0 32.5 %decode_layer.1 = bf16[1,3072]{1,0:T(2,128)(2,1)S(1)} custom-call(bf16[1,3072]{1,0:T(2,128)(2,1)} %resid_h.1, bf16[1,4096]{1,0:T(2,128)(2,1)} %query_h.1, bf16[1,4096]{1,0:T(2,128)(2,1)} %key_h.1, bf16[1,4096]{1,0:T(2,128)(2,1)} %value_h.1, f32[1,32]{1,0:T(1,128)} %bitcast.11, bf16[1,4096]{1,0:T(2,128)(2,1)} %out_gate_h.1, f32[1,4096]{1,0:T(1,128)} %bitcast.7, ...), custom_call_target="tpu_custom_call" | custom-call | tf_op jit(solution)/shard_map/decode_layer/pallas_call | solution.py:305
  32.5 0.6 %copy.17 = bf16[1,3072]{1,0:T(2,128)(2,1)} copy(bf16[1,3072]{1,0:T(2,128)(2,1)S(1)} %decode_layer.1) | data formatting | bytes 12288
